TPU v7x, 32 devices: a whole 2x2x4 slice. The times are simulated.
32 devices in a mesh: groups: 2 (over y), mp: 4 (over z), inner: 2 (over x), hst: 2 (over core).
Axes of the slice: x: 2, y: 2, z: 4, core: 2. Of those that a mesh axis runs over, the one named last changes fastest.
Arguments:
- tokens: bfloat16 [256, 8192], P(('groups', 'inner', 'hst'), 'mp'), parts along dimension 0, may hold values from -6 to 6
- query_weight: bfloat16 [8192, 8192], P('mp', 'inner'), may hold values from -0.0625 to 0.0625
- key_weight: bfloat16 [8192, 1024], P('mp', 'inner'), may hold values from -0.0625 to 0.0625
- value_weight: bfloat16 [8192, 1024], P('mp', 'inner'), may hold values from -0.0625 to 0.0625
- adapter_down_weight: bfloat16 [32, 8192, 128], P(('groups', 'mp', 'inner', 'hst')), parts along dimension 0, may hold values from -0.0625 to 0.0625
- adapter_up_weight: bfloat16 [32, 128, 1024], P(('groups', 'mp', 'inner', 'hst')), parts along dimension 0, may hold values from -0.75 to 0.75
- adapter_rank: int32 [32], P(('groups', 'mp', 'inner', 'hst')), parts along dimension 0, may hold values from 16 to 128
- row_adapter_index: int32 [256, 1], P('groups'), parts along dimension 0, may hold values from 0 to 7; in each aligned block of 32 rows (0 to 31, 32 to 63, ...) at most 8 rows name the same one
- owner_device_map: int32 [16], P('groups'), parts along dimension 0, may hold values from 0 to 7, each once
- lengths: int32 [256], P('groups'), parts along dimension 0, may hold values from 1 to 64
- page_holder_index: int32 [256, 8, 4], P('groups', 'inner'), parts along dimension 0, may hold values from 0 to 3, as said below
- page_pool_slot: int32 [256, 8, 4], P('groups', 'inner'), parts along dimension 0, may hold values from 0 to 63, as said below
- key_value_pool: bfloat16 [8, 8, 2, 64, 16, 256], P(('groups', 'mp'), 'inner', 'hst'), parts along dimension 0, may hold values from -500 to 500
Outputs:
- attended: bfloat16 [4, 64, 8192], P(('groups', 'hst'), 'mp', 'inner'), parts along dimension 0
- new_kv: bfloat16 [4, 64, 2048], P(('groups', 'hst'), 'mp', 'inner'), parts along dimension 0
There are 2 independent parts, one for each index of `groups`. A program takes and returns all parts, laid end to end along the dimension named above; an argument that names none is the same for every part. Nothing has to cross between parts.
Inputs may be any that keep to these rules, and one draw needn't show every extreme that they name: `row_adapter_index`: among the 32 rows of one input device (aligned blocks of 32 rows) no adapter is named by more than 8 rows. `owner_device_map`: each owner device index once. `page_holder_index`: for each index of hst and key-value head, every (holder, slot) holds exactly one page. Take the rows of one side in side order, in blocks of 16: the pages of one block and one key-value head lie on each holder 16 - 1 or 16 + 3 times, and 19 is reached by some holder of every block. `page_pool_slot`: slot of the page in the pool of its holder, key-value head and index of hst.
All inputs are finite; a program needn't handle non-finite values.
Results may differ from a plain program's by a relative error of at most 0.012.
The roundings to bfloat16 on the way count: a program that leaves them out, or rounds other values in their place, can miss the bound.
Values may be sent and summed in bfloat16 or wider, within the bound.
A program may use at most 128 MiB of HBM per device.

v0:
```python
import jax
import jax.numpy as jnp
from jax import lax
from jax.sharding import PartitionSpec as P

HEAD_WIDTH = 128
NPAGE = 4
PAGE = 16


THETA = 500000.0


def rotate(values, rope_angle):
    half_width = values.shape[-1] // 2
    first_half = values[..., :half_width]
    second_half = values[..., half_width:]
    cosine = jnp.cos(rope_angle)
    sine_part = jnp.sin(rope_angle)
    return jnp.concatenate(
        [
            first_half * cosine - second_half * sine_part,
            second_half * cosine + first_half * sine_part,
        ],
        axis=-1,
    )


def take_slots(pool_part, slot_table):
    return jnp.take(pool_part, slot_table, axis=0)


def on_device(
    tokens,
    query_weight,
    key_weight,
    value_weight,
    adapter_down_weight,
    adapter_up_weight,
    adapter_rank,
    row_adapter_index,
    owner_device_map,
    lengths,
    page_holder_index,
    page_pool_slot,
    key_value_pool,
):
    mp_count = lax.axis_size("mp")
    inner_count = lax.axis_size("inner")
    side_count = lax.axis_size("hst")
    mp_index = lax.axis_index("mp")
    inner_index = lax.axis_index("inner")
    side_index = lax.axis_index("hst")
    rows_home, width_part = tokens.shape
    rows_side = rows_home * inner_count
    block_rows = rows_side // mp_count
    owner_count = mp_count * inner_count
    capacity = max(2, 2 * rows_home // owner_count)
    query_cols = query_weight.shape[1]
    kv_cols = key_weight.shape[1]
    kv_local = kv_cols // HEAD_WIDTH
    full_width = width_part * mp_count
    rank_padding = adapter_down_weight.shape[2]
    delta_columns = adapter_up_weight.shape[2]
    value_start = query_cols + kv_cols
    ids_side = jnp.take(
        row_adapter_index[:, 0].reshape(inner_count, side_count, rows_home), side_index, axis=1
    )
    owner_match = ids_side[:, :, None] == jnp.arange(owner_count, dtype=jnp.int32)[None, None, :]
    owner_side = jnp.sum(jnp.where(owner_match, owner_device_map[None, None, :], 0), axis=2)
    row_order = jnp.arange(rows_home)
    same_adapter = (ids_side[:, :, None] == ids_side[:, None, :]) & (
        row_order[None, None, :] < row_order[None, :, None]
    )
    slot_place = jnp.sum(same_adapter.astype(jnp.int32), axis=2)
    owner_flat = owner_side.reshape(rows_side)
    place_flat = slot_place.reshape(rows_side)
    home_flat = jnp.arange(rows_side, dtype=jnp.int32) // rows_home
    piece_rows = lax.all_gather(tokens, "inner", axis=0, tiled=True)
    partial_value = jnp.concatenate(
        [
            jnp.dot(piece_rows, query_weight, preferred_element_type=jnp.float32),
            jnp.dot(piece_rows, key_weight, preferred_element_type=jnp.float32),
            jnp.dot(piece_rows, value_weight, preferred_element_type=jnp.float32),
        ],
        axis=1,
    )
    home_owner = lax.dynamic_index_in_dim(owner_side, inner_index, 0, keepdims=False)
    home_place = lax.dynamic_index_in_dim(slot_place, inner_index, 0, keepdims=False)
    target_slot = home_owner * capacity + home_place
    pick_rows = (jnp.arange(owner_count * capacity)[:, None] == target_slot[None, :]).astype(
        jnp.bfloat16
    )
    outgoing = jnp.dot(pick_rows, tokens, preferred_element_type=jnp.float32).astype(jnp.bfloat16)
    arrived = lax.all_to_all(
        outgoing.reshape(owner_count, capacity, width_part),
        ("mp", "inner"),
        split_axis=0,
        concat_axis=0,
        tiled=True,
    )
    owner_row_list = (
        arrived.reshape(mp_count, inner_count, capacity, width_part)
        .transpose(1, 2, 0, 3)
        .reshape(inner_count * capacity, full_width)
    )
    reduced_rows = jnp.dot(
        owner_row_list, adapter_down_weight[0], preferred_element_type=jnp.float32
    )
    rank_ceiling = adapter_rank[0]
    kept_cols = jnp.arange(rank_padding)[None, :] < rank_ceiling
    factor = rank_padding / (8.0 * rank_ceiling.astype(jnp.float32))
    reduced_rows = jnp.where(kept_cols, reduced_rows * factor, 0.0).astype(jnp.bfloat16)
    value_correction = jnp.dot(
        reduced_rows, adapter_up_weight[0], preferred_element_type=jnp.float32
    ).astype(jnp.bfloat16)
    incoming = lax.all_to_all(
        value_correction.reshape(1, inner_count, capacity, delta_columns),
        "inner",
        split_axis=3,
        concat_axis=0,
        tiled=True,
    )
    owner_mp = owner_flat // inner_count
    source_index = (owner_flat % inner_count * inner_count + home_flat) * capacity + place_flat
    picked = jnp.take(
        incoming.reshape(inner_count * inner_count * capacity, kv_cols), source_index, axis=0
    )
    extra_rows = jnp.where((owner_mp == mp_index)[:, None], picked.astype(jnp.float32), 0.0)
    partial_value = jnp.concatenate(
        [partial_value[:, :value_start], partial_value[:, value_start:] + extra_rows], axis=1
    )
    own_sums = lax.psum_scatter(partial_value, "mp", scatter_dimension=0, tiled=True)
    length_side = jnp.take(
        lengths.reshape(inner_count, side_count, rows_home), side_index, axis=1
    ).reshape(rows_side)
    my_length = lax.dynamic_slice_in_dim(length_side, mp_index * block_rows, block_rows)
    half_width = HEAD_WIDTH // 2
    inv_freq = THETA ** (-(2.0 * jnp.arange(half_width, dtype=jnp.float32)) / HEAD_WIDTH)
    rope_angle = my_length.astype(jnp.float32)[:, None, None] * inv_freq
    query_rot = rotate(
        own_sums[:, :query_cols].reshape(block_rows, query_cols // HEAD_WIDTH, HEAD_WIDTH),
        rope_angle,
    ).astype(jnp.bfloat16)
    rotated_key = rotate(
        own_sums[:, query_cols:value_start].reshape(block_rows, kv_local, HEAD_WIDTH), rope_angle
    ).astype(jnp.bfloat16)
    fresh_value = (
        own_sums[:, value_start:].reshape(block_rows, kv_local, HEAD_WIDTH).astype(jnp.bfloat16)
    )
    new_kv = jnp.concatenate([rotated_key, fresh_value], axis=2).reshape(
        1, block_rows, kv_local * 2 * HEAD_WIDTH
    )

    def side_table(table):
        picked_rows = jnp.take(
            table.reshape(inner_count, side_count, rows_home, kv_local, NPAGE), side_index, axis=1
        )
        return (
            picked_rows.reshape(mp_count, block_rows, kv_local, NPAGE)
            .transpose(0, 2, 1, 3)
            .reshape(mp_count, kv_local, block_rows * NPAGE)
        )

    holders = side_table(page_holder_index)
    slot_table = side_table(page_pool_slot)
    entries = block_rows * NPAGE
    base_count = entries // mp_count
    room_size = base_count + 3
    held_here = holders == mp_index
    held_rank = jnp.cumsum(held_here.astype(jnp.int32), axis=2) - 1
    chosen = held_here[:, :, None, :] & (
        held_rank[:, :, None, :] == jnp.arange(room_size)[None, None, :, None]
    )
    send_slot = jnp.sum(jnp.where(chosen, slot_table[:, :, None, :], 0), axis=3)
    filled = jnp.any(chosen, axis=3)
    page_pool = key_value_pool[0, :, 0]
    gathered_pages = jax.vmap(take_slots, in_axes=(0, 1), out_axes=1)(page_pool, send_slot)
    outgoing_pages = jnp.where(
        filled[:, :, :, None, None], gathered_pages, jnp.zeros((), jnp.bfloat16)
    )
    arrived_pages = lax.all_to_all(outgoing_pages, "mp", split_axis=0, concat_axis=0, tiled=True)
    my_holders = lax.dynamic_index_in_dim(holders, mp_index, 0, keepdims=False)
    holder_match = my_holders[:, :, None] == jnp.arange(mp_count, dtype=jnp.int32)[None, None, :]
    running = jnp.cumsum(holder_match.astype(jnp.int32), axis=1)
    position = jnp.sum(jnp.where(holder_match, running, 0), axis=2) - 1
    flat_index = (
        my_holders * kv_local + jnp.arange(kv_local, dtype=jnp.int32)[:, None]
    ) * room_size + position
    page_rows = jnp.take(
        arrived_pages.reshape(mp_count * kv_local * room_size, PAGE, 2 * HEAD_WIDTH),
        flat_index.reshape(-1),
        axis=0,
    )
    page_rows = page_rows.reshape(kv_local, block_rows, NPAGE * PAGE, 2 * HEAD_WIDTH)
    group_size = query_rot.shape[1] // kv_local
    query_head_group = query_rot.reshape(block_rows, kv_local, group_size, HEAD_WIDTH)
    score_scale = HEAD_WIDTH ** (-0.5)
    cache_score = (
        jnp.einsum(
            "bkgd,kbtd->bkgt",
            query_head_group,
            page_rows[..., :HEAD_WIDTH],
            preferred_element_type=jnp.float32,
        )
        * score_scale
    )
    new_score = (
        jnp.einsum(
            "njop,njp->njo", query_head_group, rotated_key, preferred_element_type=jnp.float32
        )
        * score_scale
    )
    valid_tokens = jnp.arange(NPAGE * PAGE)[None, :] < my_length[:, None]
    masked = jnp.where(valid_tokens[:, None, None, :], cache_score, -jnp.inf)
    row_top = jnp.maximum(jnp.max(masked, axis=3), new_score)
    cache_weight = jnp.exp(masked - row_top[..., None])
    new_weight = jnp.exp(new_score - row_top)
    weight_total = jnp.sum(cache_weight, axis=3) + new_weight
    cache_share = (cache_weight / weight_total[..., None]).astype(jnp.bfloat16)
    fresh_share = (new_weight / weight_total).astype(jnp.bfloat16)
    mixed = jnp.einsum(
        "bkgt,kbtd->bkgd",
        cache_share,
        page_rows[..., HEAD_WIDTH:],
        preferred_element_type=jnp.float32,
    ) + jnp.einsum("yvl,yvr->yvlr", fresh_share, fresh_value, preferred_element_type=jnp.float32)
    attended = mixed.astype(jnp.bfloat16).reshape(1, block_rows, query_cols)
    return (attended, new_kv)


def solution(mesh):
    in_specs = (
        P(("groups", "inner", "hst"), "mp"),
        P("mp", "inner"),
        P("mp", "inner"),
        P("mp", "inner"),
        P(("groups", "mp", "inner", "hst"), None, None),
        P(("groups", "mp", "inner", "hst"), None, None),
        P(("groups", "mp", "inner", "hst")),
        P("groups", None),
        P("groups"),
        P("groups"),
        P("groups", "inner", None),
        P("groups", "inner", None),
        P(("groups", "mp"), "inner", "hst", None, None, None),
    )
    out_specs = (P(("groups", "hst"), "mp", "inner"), P(("groups", "hst"), "mp", "inner"))
    return jax.shard_map(
        on_device, mesh=mesh, in_specs=in_specs, out_specs=out_specs, check_vma=False
    )
```

profile of v0, /device:TPU:0, one launch (start us, length us, event | category | flops | bytes accessed | tf_op | source)
XLA Modules:
  0.0 166.4 jit_solution(6055356080331572780)
XLA Ops:
  7.2 0.5 broadcast.507
  7.7 1.3 reduce.3
  9.2 0.7 reshape.431
  9.9 0.2 convert_reduce_fusion
  10.1 0.7 select_reduce_fusion.2
  10.8 1.8 %fusion = bf16[8,8,2048]{2,1,0:T(8,128)(2,1)} fusion(bf16[32,2048]{1,0:T(8,128)(2,1)} %param.17, s32[32]{0:T(128)S(1)} %fusion.54), kind=kOutput, calls=%fused_computation.5 | convolution fusion | flops 8521728 | bytes 393344 | tf_op jit(solution)/shard_map/dot_general | solution.py:94
  12.7 7.3 %all-to-all-start = ((bf16[8,8,2048]{2,1,0:T(8,128)(2,1)}), bf16[8,8,2048]{2,1,0:T(8,128)(2,1)}, u32[]{:S(2)}, u32[]{:S(2)}) async-start(bf16[8,8,2048]{2,1,0:T(8,128)(2,1)} %fusion), calls=%async_computation | async-start | bytes 524288 | tf_op jit(solution)/shard_map/all_to_all | solution.py:95
  19.9 0.8 reshape.446
  20.7 0.8 reshape.443
  21.6 0.1 reshape.447
  21.7 0.2 copy.72
  21.8 0.1 broadcast_in_dim.171
  22.0 0.1 reshape.444
  22.1 0.2 copy.66
  22.2 0.1 reshape.445
  22.4 1.0 reduce_window_sum.23
  23.3 1.4 select_reduce_fusion
  24.7 0.3 copy.73
  25.0 1.4 fusion.27
  26.4 5.6 %all_gather.3 = bf16[64,2048]{1,0:T(8,128)(2,1)S(1)} all-gather(bf16[32,2048]{1,0:T(8,128)(2,1)S(1)} %copy-done.3), channel_id=1, replica_groups=mesh['groups'=2,'mp'=4,'inner'=2,'hst'=2] {'inner'}, dimensions={0}, use_global_device_ids=true | all-gather | bytes 393216 | tf_op jit(solution)/shard_map/all_gather | solution.py:79
  33.1 8.9 %fusion.62 = f32[64,4096]{1,0:T(8,128)S(1)} fusion(bf16[64,2048]{1,0:T(8,128)(2,1)S(1)} %all_gather.3, bf16[2048,4096]{1,0:T(8,128)(2,1)} %param.18), kind=kOutput, calls=%fused_computation.135 | convolution fusion | flops 1073741824 | bytes 18087936 | tf_op jit(solution)/shard_map/dot_general | solution.py:82
  42.1 1.1 fusion.63
  43.2 1.2 copy.90
  44.4 0.8 copy.84
  45.2 2.2 %fusion.5 = bf16[1,2,8,1024]{3,2,1,0:T(8,128)(2,1)S(1)} fusion(bf16[16,8192]{1,0:T(8,128)(2,1)} %bitcast.109, bf16[1,8192,128]{2,1,0:T(8,128)(2,1)} %param.21, bf16[1,128,1024]{2,1,0:T(8,128)(2,1)} %param.22, f32[]{:T(128)S(6)} %div.45, pred[128]{0:T(512)(128)(4,1)S(1)} %iota_compare_fusion.7), kind=kOutput, calls=%fused_computation.16 | convolution fusion | flops 37771264 | bytes 2654340 | tf_op jit(solution)/shard_map/dot_general | solution.py:114
  47.4 1.1 copy.63
  48.5 2.2 %reshape.608 = bf16[2,2,4096]{2,1,0:T(2,128)(2,1)} reshape(bf16[1024,1,2,8]{3,2,1,0:T(2,128)(2,1)} %bitcast.107) | data formatting | bytes 65536
  50.6 3.3 %all-to-all-start.1 = ((bf16[2,2,4096]{2,1,0:T(2,128)(2,1)}), bf16[2,2,4096]{2,1,0:T(2,128)(2,1)S(1)}, u32[]{:S(2)}, u32[]{:S(2)}) async-start(bf16[2,2,4096]{2,1,0:T(2,128)(2,1)} %reshape.608), calls=%async_computation.1 | async-start | bytes 65536 | tf_op jit(solution)/shard_map/all_to_all | solution.py:117
  53.9 0.1 copy.77
  54.1 0.1 copy.76
  54.3 0.1 copy.70
  54.4 5.3 %gather_fusion.2 = bf16[304,16,256]{2,1,0:T(8,128)(2,1)} fusion(bf16[4,64,16,256]{3,2,1,0:T(8,128)(2,1)S(1)} %bitcast.102, s32[304]{0:T(512)S(1)} %reshape.582), kind=kCustom, calls=%fused_computation.2 | custom fusion | bytes 4983168 | tf_op jit(solution)/shard_map/vmap(jit(_take))/gather | solution.py:30
  59.7 1.4 reshape.609
  61.1 1.2 copy.64
  62.3 0.7 gather_fusion
  63.0 2.1 %convolution_add_fusion.1 = f32[64,512]{1,0:T(8,128)S(1)} fusion(bf16[64,2048]{1,0:T(8,128)(2,1)S(1)} %all_gather.3, bf16[2048,512]{1,0:T(8,128)(2,1)} %param.20, bf16[64,512]{1,0:T(8,128)(2,1)S(1)} %gather_fusion, pred[64]{0:T(512)(128)(4,1)S(1)} %get-tuple-element.41, pred[64]{0:T(512)(128)(4,1)S(1)} %get-tuple-element.40), kind=kOutput, calls=%fused_computation.14 | convolution fusion | flops 134348800 | bytes 2556032 | tf_op jit(solution)/shard_map/dot_general | solution.py:84
  65.1 1.2 pad_maximum_fusion
  66.3 2.1 %select_select_fusion = bf16[4,4,19,16,256]{4,3,2,0,1:T(8,128)(2,1)S(1)} fusion(bf16[4,4,19,16,256]{4,3,2,0,1:T(8,128)(2,1)} %bitcast.103, pred[4,4,19]{2,0,1:T(4,128)(4,1)S(1)} %copy.76, pred[4,4,19]{2,0,1:T(4,128)(4,1)S(1)} %copy.70), kind=kLoop, calls=%fused_computation.3 | loop fusion | flops 2490368 | bytes 4981344 | tf_op jit(solution)/shard_map/jit(_where)/select_n | solution.py:179
  68.4 1.7 %copy.78 = bf16[4,4,19,16,256]{4,3,2,1,0:T(8,128)(2,1)} copy(bf16[4,4,19,16,256]{4,3,2,0,1:T(8,128)(2,1)S(1)} %select_select_fusion) | data formatting | bytes 4980736 | tf_op jit(solution)/shard_map/jit(_where)/select_n | solution.py:179
  70.1 5.1 %all-to-all-start.2 = ((bf16[4,4,19,16,256]{4,3,2,1,0:T(8,128)(2,1)}), bf16[4,4,19,16,256]{4,3,2,1,0:T(8,128)(2,1)}, u32[]{:S(2)}, u32[]{:S(2)}) async-start(bf16[4,4,19,16,256]{4,3,2,1,0:T(8,128)(2,1)} %copy.78), calls=%async_computation.3 | async-start | bytes 4980736 | tf_op jit(solution)/shard_map/all_to_all | solution.py:182
  75.2 0.1 fusion.26
  75.3 0.1 reduce_window_sum.22
  75.5 0.2 select_reduce_fusion.1
  76.1 0.1 copy.68
  76.2 0.1 copy.67
  76.4 0.1 copy.69
  76.5 0.1 broadcast_in_dim.167
  76.6 0.1 broadcast_in_dim.168
  77.0 0.1 multiply_cosine_fusion
  77.1 44.7 %reduce-scatter.2.cloned.1.call-done = f32[16,5120]{1,0:T(8,128)} async-done(((f32[64,5120]{1,0:T(8,128)}), f32[16,5120]{1,0:T(8,128)}) %reduce-scatter.2.cloned.1.call-update) | async-done | bytes 327696 | tf_op jit(solution)/shard_map/reduce_scatter | solution.py:133
  121.8 1.0 slice_bitcast_fusion
  122.8 0.8 slice.96
  123.6 0.8 slice.69
  124.5 0.1 pad_maximum_fusion.2
  124.6 0.6 reshape.451
  125.3 0.1 fusion.22
  125.5 0.3 fusion.32
  125.7 25.7 %all-to-all-done.2 = bf16[4,4,19,16,256]{4,3,2,1,0:T(8,128)(2,1)} async-done(((bf16[4,4,19,16,256]{4,3,2,1,0:T(8,128)(2,1)}), bf16[4,4,19,16,256]{4,3,2,1,0:T(8,128)(2,1)}, u32[]{:S(2)}, u32[]{:S(2)}) %all-to-all-start.2) | async-done | bytes 2490400 | tf_op jit(solution)/shard_map/all_to_all | solution.py:182
  151.5 3.8 %gather_fusion.1 = bf16[256,16,256]{2,1,0:T(8,128)(2,1)} fusion(bf16[304,16,256]{2,1,0:T(8,128)(2,1)} %bitcast.26, s32[1024]{0:T(1024)S(1)} %pad_clamp_fusion), kind=kCustom, calls=%fused_computation.1 | custom fusion | bytes 4195328 | tf_op jit(solution)/shard_map/jit(_take)/gather | solution.py:190
  155.2 1.9 %copy_select_fusion = bf16[4,16,64,256]{3,2,0,1:T(8,128)(2,1)S(1)} fusion(bf16[4,16,64,256]{3,2,1,0:T(8,128)(2,1)} %bitcast.105, pred[4,16,64]{2,0,1:T(4,128)(4,1)S(1)} %broadcast_in_dim.168), kind=kLoop, calls=%fused_computation.8 | loop fusion | flops 1048576 | bytes 4198400 | tf_op jit(solution)/shard_map/jit(_take)/select_n | solution.py:190
  157.2 0.8 fusion.61
  158.0 0.3 fusion.20
  158.3 0.5 fusion.4
  158.8 0.7 reshape.450
  (55 shorter events, 1.8 us)
Async XLA Ops:
  7.2 47.2 %copy-start = (bf16[1,4,1,64,16,256]{5,4,3,2,1,0:T(8,128)(2,1)S(1)}, bf16[1,4,1,64,16,256]{5,4,3,2,1,0:T(8,128)(2,1)}, u32[]{:S(2)}) copy-start(bf16[1,4,1,64,16,256]{5,4,3,2,1,0:T(8,128)(2,1)} %param.29) | copy-start | bytes 6291460
  7.2 19.2 %copy-start.3 = (bf16[32,2048]{1,0:T(8,128)(2,1)S(1)}, bf16[32,2048]{1,0:T(8,128)(2,1)}, u32[]{:S(2)}) copy-start(bf16[32,2048]{1,0:T(8,128)(2,1)} %param.17) | copy-start | bytes 393220
  12.7 30.6 %all-to-all-start = ((bf16[8,8,2048]{2,1,0:T(8,128)(2,1)}), bf16[8,8,2048]{2,1,0:T(8,128)(2,1)}, u32[]{:S(2)}, u32[]{:S(2)}) async-start(bf16[8,8,2048]{2,1,0:T(8,128)(2,1)} %fusion), calls=%async_computation | async-start | bytes 524288 | tf_op jit(solution)/shard_map/all_to_all | solution.py:95
  33.1 9.0 %copy-start.1 = (bf16[2048,512]{1,0:T(8,128)(2,1)S(1)}, bf16[2048,512]{1,0:T(8,128)(2,1)}, u32[]{:S(2)}) copy-start(bf16[2048,512]{1,0:T(8,128)(2,1)} %param.19) | copy-start | bytes 6291460
  50.6 9.0 %all-to-all-start.1 = ((bf16[2,2,4096]{2,1,0:T(2,128)(2,1)}), bf16[2,2,4096]{2,1,0:T(2,128)(2,1)S(1)}, u32[]{:S(2)}, u32[]{:S(2)}) async-start(bf16[2,2,4096]{2,1,0:T(2,128)(2,1)} %reshape.608), calls=%async_computation.1 | async-start | bytes 65536 | tf_op jit(solution)/shard_map/all_to_all | solution.py:117
  53.9 67.9 %reduce-scatter.2.cloned.1.call-start = ((), (), s32[]{:S(2)}) async-start(), calls=%async_computation.4 | async-start | bytes 1638400 | tf_op jit(solution)/shard_map/reduce_scatter | solution.py:133
  63.0 2.1 %copy-start.2 = (f32[64,512]{1,0:T(8,128)S(1)}, f32[64,512]{1,0:T(8,128)}, u32[]{:S(2)}) copy-start(f32[64,512]{1,0:T(8,128)} %fusion.63) | copy-start | bytes 393220
  70.1 81.3 %all-to-all-start.2 = ((bf16[4,4,19,16,256]{4,3,2,1,0:T(8,128)(2,1)}), bf16[4,4,19,16,256]{4,3,2,1,0:T(8,128)(2,1)}, u32[]{:S(2)}, u32[]{:S(2)}) async-start(bf16[4,4,19,16,256]{4,3,2,1,0:T(8,128)(2,1)} %copy.78), calls=%async_computation.3 | async-start | bytes 4980736 | tf_op jit(solution)/shard_map/all_to_all | solution.py:182
Sparse Core Ops, SparseCore 0:
  66.4 55.3 reduce-scatter.1
where the time goes:
time: 167 us; the launch traced here: 166 us
  waiting for transfers between devices  70.4 us (42%)
  local copies, waits for them, and re-layouts  29 us (17%)
  matrix products  17.7 us (11%)
  starting transfers between devices  15.6 us (9%)
  between operations  15.1 us (9%)
  other arithmetic  12.9 us (8%)
  blocking collectives  5.64 us (3%)
    reduce_scatter x1, waiting for transfers between devices, on_device(): lax.psum_scatter(partial_value, 'mp', scatter_dimension=0, tiled=True)  44.7 us
    all_to_all x1, waiting for transfers between devices, on_device(): lax.all_to_all(outgoing_pages, 'mp', split_axis=0, concat_axis=0, tiled=T...  25.7 us
    dot_general x1, matrix products, on_device(): jnp.dot(piece_rows, query_weight, preferred_element_type=jnp.float32)  8.93 us
    all_to_all x1, starting transfers between devices, on_device(): lax.all_to_all(outgoing.reshape(owner_count, capacity, width_part), ('mp'...  7.25 us
    unnamed x14, local copies, waits for them, and re-layouts  5.96 us
    all_gather x1, blocking collectives, on_device(): piece_rows = lax.all_gather(tokens, 'inner', axis=0, tiled=True)  5.64 us
    gather x3, local copies, waits for them, and re-layouts, take_slots(): return jnp.take(pool_part, slot_table, axis=0)  5.45 us
    all_to_all x1, starting transfers between devices, on_device(): lax.all_to_all(outgoing_pages, 'mp', split_axis=0, concat_axis=0, tiled=T...  5.09 us
  transfers between devices with their start and end apart: 4, of which 2 were waited for; matrix products, arithmetic and copies ran while one was open for 19% of the time, Pallas kernels for 0%

commit v1 on v0

v1 whole, which is shorter than its diff:
```python
import functools

import jax
import jax.numpy as jnp
from jax import lax
from jax.experimental import pallas as pl
from jax.experimental.pallas import tpu as pltpu
from jax.sharding import PartitionSpec as P

HEAD_WIDTH = 128
NPAGE = 4
PAGE = 16
THETA = 500000.0
MESH = pl.DeviceIdType.MESH
PARTIAL = jnp.float32
BACK = jnp.bfloat16


def kernel(
    dims,
    tokens,
    wq,
    wk,
    wv,
    down,
    up,
    rank,
    table,
    omap,
    rope,
    pool,
    attended,
    new_kv,
    x_all,
    lo,
    lr,
    wq_v,
    wk_v,
    wv_v,
    down_v,
    up_v,
    pool_v,
    part,
    rs_in,
    partkv,
    rskv,
    q_all,
    bias,
    s_buf,
    p_buf,
    ao,
    st,
    ain,
    sin,
    dl_out,
    dl_in,
    rot,
    local_sem,
    x_send,
    x_recv,
    l_send,
    l_recv,
    d_send,
    d_recv,
    kv_send,
    kv_recv,
    r_send,
    r_recv,
    q_send,
    q_recv,
    a_send,
    a_recv,
    t_send,
    t_recv,
):
    MP, IN, SD = dims
    m = lax.axis_index("mp")
    i = lax.axis_index("inner")
    h = lax.axis_index("hst")
    R, W = tokens.shape
    RS = R * IN
    B = RS // MP
    K, _, QW = wq_v.shape
    KC = wk_v.shape[1]
    G = QW // HEAD_WIDTH
    SLOTS = pool_v.shape[1]
    T = SLOTS * PAGE
    OC = MP * IN
    CAP = max(2, 2 * R // OC)
    L = IN * CAP
    f32 = jnp.float32
    bf16 = jnp.bfloat16
    scale = HEAD_WIDTH ** (-0.5)

    def peer_of(d):
        return lax.rem(m + d, MP)

    def source_of(d):
        return lax.rem(m + MP - d, MP)

    def ipeer(d):
        return lax.rem(i + d, IN)

    def isource(d):
        return lax.rem(i + IN - d, IN)

    def remote(src, dst, ssem, rsem, axis, dev):
        return pltpu.make_async_remote_copy(
            src_ref=src,
            dst_ref=dst,
            send_sem=ssem,
            recv_sem=rsem,
            device_id={axis: dev},
            device_id_type=MESH,
        )

    barrier = pltpu.get_barrier_semaphore()
    for d in range(1, MP):
        pl.semaphore_signal(barrier, inc=1, device_id={"mp": peer_of(d)}, device_id_type=MESH)
    for d in range(1, IN):
        pl.semaphore_signal(barrier, inc=1, device_id={"inner": ipeer(d)}, device_id_type=MESH)

    loads = []
    for k in range(K):
        loads.append(
            pltpu.make_async_copy(wq.at[:, pl.ds(k * QW, QW)], wq_v.at[k], local_sem.at[k])
        )
    loads.append(pltpu.make_async_copy(wk, wk_v, local_sem.at[K]))
    loads.append(pltpu.make_async_copy(wv, wv_v, local_sem.at[K + 1]))
    loads.append(pltpu.make_async_copy(down.at[0], down_v, local_sem.at[K + 2]))
    loads.append(pltpu.make_async_copy(up.at[0], up_v, local_sem.at[K + 3]))
    loads.append(pltpu.make_async_copy(pool.at[0, :, 0], pool_v, local_sem.at[K + 4]))
    for c in loads:
        c.start()

    pl.semaphore_wait(barrier, MP - 1 + IN - 1)

    sends = []
    for d in range(1, IN):
        c = remote(tokens, x_all.at[i], x_send.at[d], x_recv.at[d], "inner", ipeer(d))
        c.start()
        sends.append(c)
    x_all[i] = tokens[...]

    def side_rows(ref, lo_, width):
        return jnp.concatenate(
            [ref[pl.ds((j * SD + h) * R, R), lo_ : lo_ + width] for j in range(IN)], axis=0
        )

    NT = K * NPAGE
    tab = side_rows(table, 0, NT + 2)
    len_c = tab[:, NT : NT + 1]
    ids_c = tab[:, NT + 1 : NT + 2]
    rows_a = lax.broadcasted_iota(jnp.int32, (RS, RS), 0)
    rows_b = lax.broadcasted_iota(jnp.int32, (RS, RS), 1)
    ids_f = ids_c.astype(f32)
    ids_r = jnp.sum(jnp.where(rows_a == rows_b, ids_f, 0.0), axis=0, keepdims=True)
    same = (ids_f == ids_r) & (rows_a // R == rows_b // R)
    own_iota = lax.broadcasted_iota(jnp.int32, (RS, OC), 1)
    owner_c = jnp.sum(
        jnp.where(own_iota == ids_c, omap[...].astype(f32), 0.0), axis=1, keepdims=True
    )
    owner_r = jnp.sum(jnp.where(rows_a == rows_b, owner_c, 0.0), axis=0, keepdims=True)
    home_c = (lax.broadcasted_iota(jnp.int32, (RS, 1), 0) // R * CAP).astype(f32)
    home_r = (lax.broadcasted_iota(jnp.int32, (1, RS), 1) // R * CAP).astype(f32)
    place_c = home_c + jnp.sum(
        jnp.where(same & (rows_b < rows_a), 1.0, 0.0), axis=1, keepdims=True
    )
    place_r = home_r + jnp.sum(
        jnp.where(same & (rows_a < rows_b), 1.0, 0.0), axis=0, keepdims=True
    )

    for d in range(1, IN):
        remote(tokens, x_all.at[isource(d)], x_send.at[d], x_recv.at[d], "inner", ipeer(d)).wait_recv()
    x = x_all[...].reshape(RS, W)

    q_iota = lax.broadcasted_iota(jnp.int32, (L, RS), 0).astype(f32)
    for dest in range(MP):
        target = (dest * IN + i).astype(f32)
        pick = jnp.where((owner_r == target) & (place_r == q_iota), 1.0, 0.0).astype(bf16)
        lo[dest] = jnp.dot(pick, x, preferred_element_type=f32).astype(bf16)
    for d in range(1, MP):
        c = remote(lo.at[peer_of(d)], lr.at[m], l_send.at[d], l_recv.at[d], "mp", peer_of(d))
        c.start()
        sends.append(c)
    lr[m] = lo[m]

    for k in range(K):
        loads[k].wait()
        y = jnp.dot(x, wq_v[k], preferred_element_type=f32)
        part[k] = y.reshape(MP, B, QW).astype(part.dtype)
        for d in range(1, MP):
            c = remote(
                part.at[k, peer_of(d)], rs_in.at[k, d], r_send.at[k, d], r_recv.at[k, d], "mp", peer_of(d)
            )
            c.start()
            sends.append(c)

    col = lax.broadcasted_iota(jnp.int32, (RS, T), 1)
    for k in range(K):
        live = jnp.zeros((RS, T), f32)
        for p in range(NPAGE):
            slot = tab[:, k * NPAGE + p : k * NPAGE + p + 1]
            first = slot * PAGE
            last = first + jnp.where(slot >= 0, jnp.minimum(PAGE, len_c - p * PAGE), 0)
            live = jnp.where((col >= first) & (col < last), 1.0, live)
        bias[k] = jnp.where(live > 0.0, 0.0, -1e30)

    loads[K + 2].wait()
    loads[K + 3].wait()
    for d in range(1, MP):
        remote(
            lo.at[peer_of(d)], lr.at[source_of(d)], l_send.at[d], l_recv.at[d], "mp", peer_of(d)
        ).wait_recv()
    reduced = jnp.zeros((L, down_v.shape[1]), f32)
    for j in range(MP):
        reduced = reduced + jnp.dot(
            lr[j], down_v[j * W : (j + 1) * W, :], preferred_element_type=f32
        )
    rank_now = rank[0]
    pad = down_v.shape[1]
    kept = lax.broadcasted_iota(jnp.int32, (L, pad), 1) < rank_now
    factor = pad / (8.0 * jnp.full((L, pad), rank_now, jnp.int32).astype(f32))
    shrunk = jnp.where(kept, reduced * factor, 0.0).astype(bf16)
    delta = jnp.dot(shrunk, up_v[...], preferred_element_type=f32).astype(bf16)
    for j in range(IN):
        dl_out[j] = delta[:, j * KC : (j + 1) * KC]
    for d in range(1, IN):
        c = remote(dl_out.at[ipeer(d)], dl_in.at[i], d_send.at[d], d_recv.at[d], "inner", ipeer(d))
        c.start()
        sends.append(c)
    dl_in[i] = dl_out[i]

    for j in range(IN):
        rot[pl.ds(j * R, R), :] = rope[pl.ds((j * SD + h) * R, R), :]
    mine = pl.multiple_of(m * B, B)
    rot_c = rot[pl.ds(mine, B), 0:HEAD_WIDTH]
    rot_s = rot[pl.ds(mine, B), HEAD_WIDTH : 2 * HEAD_WIDTH]

    def turn(u):
        return (u * rot_c + pltpu.roll(u, HEAD_WIDTH // 2, 1) * rot_s).astype(bf16)

    for k in range(K):
        for d in range(1, MP):
            remote(
                part.at[k, peer_of(d)], rs_in.at[k, d], r_send.at[k, d], r_recv.at[k, d], "mp", peer_of(d)
            ).wait_recv()
        for g in range(G):
            cut = slice(g * HEAD_WIDTH, (g + 1) * HEAD_WIDTH)
            total = part[k, m, :, cut].astype(f32)
            for d in range(1, MP):
                total = total + rs_in[k, d, :, cut].astype(f32)
            q_all[k, m, :, cut] = turn(total)
        for d in range(1, MP):
            c = remote(
                q_all.at[k, m], q_all.at[k, m], q_send.at[k, d], q_recv.at[k, d], "mp", peer_of(d)
            )
            c.start()
            sends.append(c)

    loads[K].wait()
    loads[K + 1].wait()
    partkv[:, :, 0:KC] = jnp.dot(x, wk_v[...], preferred_element_type=f32).reshape(MP, B, KC)
    vsum = jnp.dot(x, wv_v[...], preferred_element_type=f32)
    for d in range(1, IN):
        remote(
            dl_out.at[ipeer(d)], dl_in.at[isource(d)], d_send.at[d], d_recv.at[d], "inner", ipeer(d)
        ).wait_recv()
    l_iota = lax.broadcasted_iota(jnp.int32, (RS, L), 1).astype(f32)
    for j in range(IN):
        target = (m * IN + j).astype(f32)
        back = jnp.where((owner_c == target) & (place_c == l_iota), 1.0, 0.0).astype(bf16)
        vsum = vsum + jnp.dot(back, dl_in[j], preferred_element_type=f32)
    partkv[:, :, KC : 2 * KC] = vsum.reshape(MP, B, KC)
    for d in range(1, MP):
        c = remote(
            partkv.at[peer_of(d)], rskv.at[d], kv_send.at[d], kv_recv.at[d], "mp", peer_of(d)
        )
        c.start()
        sends.append(c)

    loads[K + 4].wait()
    lane = lax.broadcasted_iota(jnp.int32, (RS, HEAD_WIDTH), 1)
    for k in range(K):
        for d in range(1, MP):
            remote(
                q_all.at[k, m], q_all.at[k, source_of(d)], q_send.at[k, d], q_recv.at[k, d], "mp", peer_of(d)
            ).wait_recv()
        queries = jnp.concatenate(
            [
                q_all[k, :, :, g * HEAD_WIDTH : (g + 1) * HEAD_WIDTH].reshape(RS, HEAD_WIDTH)
                for g in range(G)
            ],
            axis=0,
        )
        keys = pool_v[k, :, :, 0:HEAD_WIDTH].reshape(T, HEAD_WIDTH)
        values = pool_v[k, :, :, HEAD_WIDTH : 2 * HEAD_WIDTH].reshape(T, HEAD_WIDTH)
        s_buf[...] = lax.dot_general(
            queries, keys, (((1,), (1,)), ((), ())), preferred_element_type=f32
        )
        stat = jnp.zeros((RS, HEAD_WIDTH), f32)
        for g in range(G):
            s = s_buf[g * RS : (g + 1) * RS, :] * scale + bias[k]
            top = jnp.max(s, axis=1, keepdims=True)
            e = jnp.exp(s - top)
            p_buf[g * RS : (g + 1) * RS, :] = e.astype(bf16)
            stat = jnp.where(lane == g, top, stat)
            stat = jnp.where(lane == G + g, jnp.sum(e, axis=1, keepdims=True), stat)
        mixed = jnp.dot(p_buf[...], values, preferred_element_type=f32)
        for g in range(G):
            ao[k, :, :, g * HEAD_WIDTH : (g + 1) * HEAD_WIDTH] = (
                mixed[g * RS : (g + 1) * RS, :].reshape(MP, B, HEAD_WIDTH).astype(ao.dtype)
            )
        st[k] = stat.reshape(MP, B, HEAD_WIDTH)
        for d in range(1, MP):
            c = remote(ao.at[k, peer_of(d)], ain.at[k, d], a_send.at[k, d], a_recv.at[k, d], "mp", peer_of(d))
            c.start()
            sends.append(c)
            c = remote(st.at[k, peer_of(d)], sin.at[k, d], t_send.at[k, d], t_recv.at[k, d], "mp", peer_of(d))
            c.start()
            sends.append(c)

    for d in range(1, MP):
        remote(
            partkv.at[peer_of(d)], rskv.at[d], kv_send.at[d], kv_recv.at[d], "mp", peer_of(d)
        ).wait_recv()
    kv = partkv[m]
    for d in range(1, MP):
        kv = kv + rskv[d]
    fresh_key = []
    fresh_value = []
    for k in range(K):
        key = turn(kv[:, k * HEAD_WIDTH : (k + 1) * HEAD_WIDTH])
        value = kv[:, KC + k * HEAD_WIDTH : KC + (k + 1) * HEAD_WIDTH].astype(bf16)
        new_kv[0, :, 2 * k * HEAD_WIDTH : (2 * k + 1) * HEAD_WIDTH] = key
        new_kv[0, :, (2 * k + 1) * HEAD_WIDTH : (2 * k + 2) * HEAD_WIDTH] = value
        fresh_key.append(key.astype(f32))
        fresh_value.append(value.astype(f32))

    for k in range(K):
        for d in range(1, MP):
            remote(
                ao.at[k, peer_of(d)], ain.at[k, d], a_send.at[k, d], a_recv.at[k, d], "mp", peer_of(d)
            ).wait_recv()
            remote(
                st.at[k, peer_of(d)], sin.at[k, d], t_send.at[k, d], t_recv.at[k, d], "mp", peer_of(d)
            ).wait_recv()
        stats = [st[k, m]] + [sin[k, d] for d in range(1, MP)]
        for g in range(G):
            cut = slice(g * HEAD_WIDTH, (g + 1) * HEAD_WIDTH)
            query = q_all[k, m, :, cut].astype(f32)
            fresh = jnp.sum(query * fresh_key[k], axis=1, keepdims=True) * scale
            top = fresh
            for s in stats:
                top = jnp.maximum(top, s[:, g : g + 1])
            shares = [jnp.exp(s[:, g : g + 1] - top) for s in stats]
            fresh_weight = jnp.exp(fresh - top)
            total = fresh_weight
            for s, share in zip(stats, shares):
                total = total + s[:, G + g : G + g + 1] * share
            out = (fresh_weight / total).astype(bf16).astype(f32) * fresh_value[k]
            out = out + (shares[0] / total) * ao[k, m, :, cut].astype(f32)
            for d in range(1, MP):
                out = out + (shares[d] / total) * ain[k, d, :, cut].astype(f32)
            start = k * QW + g * HEAD_WIDTH
            attended[0, :, start : start + HEAD_WIDTH] = out.astype(bf16)

    for c in sends:
        c.wait_send()


def on_device(
    dims,
    tokens,
    query_weight,
    key_weight,
    value_weight,
    adapter_down_weight,
    adapter_up_weight,
    adapter_rank,
    row_adapter_index,
    owner_device_map,
    lengths,
    page_holder_index,
    page_pool_slot,
    key_value_pool,
):
    MP, IN, SD = dims
    R, W = tokens.shape
    RS = R * IN
    B = RS // MP
    QC = query_weight.shape[1]
    KC = key_weight.shape[1]
    K = KC // HEAD_WIDTH
    QW = QC // K
    G = QW // HEAD_WIDTH
    OC = MP * IN
    CAP = max(2, 2 * R // OC)
    L = IN * CAP
    pad = adapter_down_weight.shape[2]
    delta_columns = adapter_up_weight.shape[2]
    slots = key_value_pool.shape[3]
    T = slots * PAGE
    N = lengths.shape[0]
    bf16 = jnp.bfloat16
    f32 = jnp.float32

    held = jnp.where(page_holder_index == lax.axis_index("mp"), page_pool_slot, -1)
    table = jnp.concatenate(
        [held.reshape(N, K * NPAGE), lengths[:, None], row_adapter_index], axis=1
    )
    half = HEAD_WIDTH // 2
    inv_freq = THETA ** (-(2.0 * jnp.arange(half, dtype=f32)) / HEAD_WIDTH)
    angle = lengths.astype(f32)[:, None] * inv_freq
    cosine, sine = jnp.cos(angle), jnp.sin(angle)
    rope = jnp.concatenate([cosine, cosine, -sine, sine], axis=1)

    vmem = pl.BlockSpec(memory_space=pltpu.VMEM)
    hbm = pl.BlockSpec(memory_space=pl.ANY)
    DMA = pltpu.SemaphoreType.DMA
    return pl.pallas_call(
        functools.partial(kernel, dims),
        out_shape=(
            jax.ShapeDtypeStruct((1, B, QC), bf16),
            jax.ShapeDtypeStruct((1, B, 2 * KC), bf16),
        ),
        in_specs=[
            vmem,
            hbm,
            hbm,
            hbm,
            hbm,
            hbm,
            pl.BlockSpec(memory_space=pltpu.SMEM),
            vmem,
            vmem,
            vmem,
            hbm,
        ],
        out_specs=(vmem, vmem),
        scratch_shapes=[
            pltpu.VMEM((IN, R, W), bf16),
            pltpu.VMEM((MP, L, W), bf16),
            pltpu.VMEM((MP, L, W), bf16),
            pltpu.VMEM((K, W, QW), bf16),
            pltpu.VMEM((W, KC), bf16),
            pltpu.VMEM((W, KC), bf16),
            pltpu.VMEM((MP * W, pad), bf16),
            pltpu.VMEM((pad, delta_columns), bf16),
            pltpu.VMEM((K, slots, PAGE, 2 * HEAD_WIDTH), bf16),
            pltpu.VMEM((K, MP, B, QW), PARTIAL),
            pltpu.VMEM((K, MP, B, QW), PARTIAL),
            pltpu.VMEM((MP, B, 2 * KC), f32),
            pltpu.VMEM((MP, B, 2 * KC), f32),
            pltpu.VMEM((K, MP, B, QW), bf16),
            pltpu.VMEM((K, RS, T), f32),
            pltpu.VMEM((G * RS, T), f32),
            pltpu.VMEM((G * RS, T), bf16),
            pltpu.VMEM((K, MP, B, QW), BACK),
            pltpu.VMEM((K, MP, B, HEAD_WIDTH), f32),
            pltpu.VMEM((K, MP, B, QW), BACK),
            pltpu.VMEM((K, MP, B, HEAD_WIDTH), f32),
            pltpu.VMEM((IN, L, KC), bf16),
            pltpu.VMEM((IN, L, KC), bf16),
            pltpu.VMEM((RS, 2 * HEAD_WIDTH), f32),
            DMA((K + 5,)),
            DMA((IN,)),
            DMA((IN,)),
            DMA((MP,)),
            DMA((MP,)),
            DMA((IN,)),
            DMA((IN,)),
            DMA((MP,)),
            DMA((MP,)),
            DMA((K, MP)),
            DMA((K, MP)),
            DMA((K, MP)),
            DMA((K, MP)),
            DMA((K, MP)),
            DMA((K, MP)),
            DMA((K, MP)),
            DMA((K, MP)),
        ],
        compiler_params=pltpu.CompilerParams(
            collective_id=0, has_side_effects=True, vmem_limit_bytes=56 * 1024 * 1024
        ),
    )(
        tokens,
        query_weight,
        key_weight,
        value_weight,
        adapter_down_weight,
        adapter_up_weight,
        adapter_rank,
        table,
        owner_device_map.reshape(1, OC),
        rope,
        key_value_pool,
    )


def solution(mesh):
    in_specs = (
        P(("groups", "inner", "hst"), "mp"),
        P("mp", "inner"),
        P("mp", "inner"),
        P("mp", "inner"),
        P(("groups", "mp", "inner", "hst"), None, None),
        P(("groups", "mp", "inner", "hst"), None, None),
        P(("groups", "mp", "inner", "hst")),
        P("groups", None),
        P("groups"),
        P("groups"),
        P("groups", "inner", None),
        P("groups", "inner", None),
        P(("groups", "mp"), "inner", "hst", None, None, None),
    )
    out_specs = (P(("groups", "hst"), "mp", "inner"), P(("groups", "hst"), "mp", "inner"))
    dims = (mesh.shape["mp"], mesh.shape["inner"], mesh.shape["hst"])
    return jax.shard_map(
        functools.partial(on_device, dims),
        mesh=mesh,
        in_specs=in_specs,
        out_specs=out_specs,
        check_vma=False,
    )
```

time: 167 us -> 82 us (0.49)
  Pallas kernels: 0 us -> 73.5 us
  waiting for transfers between devices: 70.4 us -> 0 us
  local copies, waits for them, and re-layouts: 29 us -> 3.67 us
  matrix products: 17.7 us -> 0 us
  starting transfers between devices: 15.6 us -> 0 us
  between operations: 15.1 us -> 1.3 us
  other arithmetic: 12.9 us -> 3.16 us
  blocking collectives: 5.64 us -> 0 us
    pallas_call x0 -> x1, Pallas kernels: none -> 73.5 us  [on_device(): pl.pallas_call(functools.partial(kernel, dims), out_shape=(jax.ShapeDtype...]
    reduce_scatter x1 -> x0, waiting for transfers between devices: 44.7 us -> none  [on_device(): lax.psum_scatter(partial_value, 'mp', scatter_dimension=0, tiled=True)]
    all_to_all x3 -> x0, waiting for transfers between devices: 25.7 us -> none  [the longest x1 25.7 us: on_device(): lax.all_to_all(outgoing_pages, 'mp', split_axis=0, concat_axis=0, tiled=T...]
    dot_general x8 -> x0, matrix products: 17.7 us -> none  [the longest x1 8.93 us: on_device(): jnp.dot(piece_rows, query_weight, preferred_element_type=jnp.float32)]
    all_to_all x3 -> x0, starting transfers between devices: 15.6 us -> none  [the longest x1 7.25 us: on_device(): lax.all_to_all(outgoing.reshape(owner_count, capacity, width_part), ('mp'...]
    gather x5 -> x0, local copies, waits for them, and re-layouts: 9.92 us -> none  [the longest x3 5.45 us: take_slots(): return jnp.take(pool_part, slot_table, axis=0)]
    all_gather x1 -> x0, blocking collectives: 5.64 us -> none  [on_device(): piece_rows = lax.all_gather(tokens, 'inner', axis=0, tiled=True)]
    reshape x15 -> x0, local copies, waits for them, and re-layouts: 5.47 us -> none  [the longest x2 1.58 us: side_table(): table.reshape(inner_count, side_count, rows_home, kv_local, NPAGE)]
  transfers between devices with their start and end apart: 4 -> 0, of which waited for: 2 -> 0; matrix products, arithmetic and copies ran while one was open for 19% -> 0% of each run, Pallas kernels for 0% -> 0%
where the time goes in v1:
time: 82 us; the launch traced here: 81.7 us
  Pallas kernels  73.5 us (90%)
  local copies, waits for them, and re-layouts  3.67 us (4%)
  other arithmetic  3.16 us (4%)
  between operations  1.3 us (2%)
    pallas_call x1, Pallas kernels, on_device(): pl.pallas_call(functools.partial(kernel, dims), out_shape=(jax.ShapeDtype...  73.5 us
    unnamed x2, local copies, waits for them, and re-layouts  2.94 us

profile of v1, /device:TPU:0, one launch (start us, length us, event | category | flops | bytes accessed | tf_op | source)
XLA Modules:
  0.0 81.7 jit_solution(11221632008776073975)
XLA Ops:
  0.6 0.7 convert_element_type.3
  1.3 0.3 multiply_cosine_fusion
  1.6 0.8 pad_maximum_fusion.rope
  2.4 0.7 compare_select_fusion
  3.1 0.7 pad_add_fusion
  3.8 0.7 copy.23.table
  5.2 73.5 %shard_map.140 = (bf16[1,16,4096]{2,1,0:T(8,128)(2,1)}, bf16[1,16,1024]{2,1,0:T(8,128)(2,1)}) custom-call(bf16[32,2048]{1,0:T(8,128)(2,1)} %tokens.1, bf16[2048,4096]{1,0:T(8,128)(2,1)} %wq.1, bf16[2048,512]{1,0:T(8,128)(2,1)} %wk.1, bf16[2048,512]{1,0:T(8,128)(2,1)} %wv.1, bf16[1,8192,128]{2,1,0:T(8,128)(2,1)} %down.1, bf16[1,128,1024]{2,1,0:T(8,128)(2,1)} %up.1, ...), custom_call_target="tpu_custom_call" | custom-call | tf_op jit(solution)/shard_map/pallas_call | solution.py:421
  78.7 1.6 %copy.27 = bf16[1,16,4096]{2,1,0:T(8,128)(2,1)} copy(bf16[1,16,4096]{2,1,0:T(8,128)(2,1)} %get-tuple-element.7) | data formatting | bytes 262144
  80.3 1.4 %copy.28 = bf16[1,16,1024]{2,1,0:T(8,128)(2,1)} copy(bf16[1,16,1024]{2,1,0:T(8,128)(2,1)} %get-tuple-element.8) | data formatting | bytes 65536
  (1 shorter events, 0.0 us)
